TPU v7x, 512 devices: a whole 4x8x8 slice. The times are simulated.
512 devices in a mesh: row: 16 (over y, x_lo), col: 32 (over x_hi, z, core).
Axes of the slice: x: 4 (x_hi: 2, x_lo: 2; x = x_hi * 2 + x_lo), y: 8, z: 8, core: 2. Of those that a mesh axis runs over, the one named last changes fastest.
Arguments:
- tokens: bfloat16 [65536, 3584], P(('row', 'col')), may hold values from -6 to 6
- targets: bfloat16 [65536, 3584], P(('row', 'col')), may hold values from -6 to 6
- w_up: bfloat16 [32, 3584, 448], P('col', 'row'), may hold values from -6 to 6
- w_down: bfloat16 [16, 3584, 448], P('row', 'col'), may hold values from -6 to 6
- up_momentum: float32 [32, 3584, 448], P('col', 'row'), may hold values from -2 to 2
- down_momentum: float32 [16, 3584, 448], P('row', 'col'), may hold values from -2 to 2
- member_up: int32 [16, 32], replicated, may hold values from 0 to 1, as said below
- member_down: int32 [16, 32], replicated, may hold values from 0 to 1, as said below
- path_rate: float32 [16, 32], replicated, may hold values from 0.1 to 1
Outputs:
- new_up: bfloat16 [32, 3584, 448], P('col', 'row')
- new_up_momentum: float32 [32, 3584, 448], P('col', 'row')
- new_down: bfloat16 [16, 3584, 448], P('row', 'col')
- new_down_momentum: float32 [16, 3584, 448], P('row', 'col')
Inputs may be any that keep to these rules, and one draw needn't show every extreme that they name: Every column of member_up holds at least one 1. Every row of member_down holds at least one 1.
All inputs are finite; a program needn't handle non-finite values. Where the computation divides by a largest or mean magnitude, that divisor is 1e-20 or more.
Results may differ from a plain program's by a relative error of at most 0.006.
Values may be sent and summed in bfloat16 or wider, within the bound.
A program may use at most 64 MiB of HBM per device.

v0:
```python
import jax
import jax.numpy as jnp
from jax import lax
from jax.sharding import Mesh
from jax.sharding import PartitionSpec as P

ROW = ("row_0", "row_1")
ROW_COL = ("row_0", "row_1", "col")


def gathered_by_axis(x, axes, dim):
    filled = x
    for number in range(len(axes) - 1, -1, -1):
        filled = lax.all_gather(filled, axes[number], axis=dim, tiled=True)
    return filled


def joined_along(parts, dim):
    parts = jnp.moveaxis(parts, 0, dim)
    shape = parts.shape
    return parts.reshape(*shape[:dim], shape[dim] * shape[dim + 1], *shape[dim + 2 :])


def from_everyone(x, axis):
    peers = lax.axis_size(axis)
    return lax.all_to_all(jnp.broadcast_to(x[None], (peers, *x.shape)), axis, 0, 0, tiled=True)


def collect(x, axis, dim):
    return joined_along(from_everyone(x, axis), dim)


def silu_slope(pre):
    sig = jax.nn.sigmoid(pre)
    return sig * (1.0 + pre * (1.0 - sig))


def finish_forward(tokens, targets, pre, down_whole, inv_hidden):
    hidden_act = jax.nn.silu(pre).astype(jnp.bfloat16)
    mixed = (
        lax.dot_general(
            hidden_act, down_whole, (((1,), (1,)), ((), ())), preferred_element_type=jnp.float32
        )
        * inv_hidden
    )
    slope_out = (tokens.astype(jnp.float32) + mixed - targets.astype(jnp.float32)).astype(
        jnp.bfloat16
    )
    return (hidden_act, slope_out)


def packed(grad, rate):
    spread = jnp.sqrt(jnp.mean(grad * grad, axis=-1, keepdims=True) + 1e-05)
    unit = grad / (jnp.abs(grad) + spread)
    largest = jnp.max(jnp.abs(unit), axis=-1, keepdims=True) + 1e-06
    return ((unit / largest).astype(jnp.bfloat16), rate * largest[..., 0])


def owner_sum(weights, pieces):
    quant, scales = pieces
    factor = weights[:, None] * scales
    return jnp.sum(factor[:, :, None] * quant.astype(jnp.float32), axis=0)


def per_device(
    tokens, targets, w_up, w_down, up_momentum, down_momentum, member_up, member_down, path_rate
):
    width = tokens.shape[1]
    hidden = w_up.shape[2]
    rows = tokens.shape[0]
    inv_width = width ** (-0.5)
    inv_hidden = hidden ** (-0.5)
    row_index = lax.axis_index(ROW)
    col_index = lax.axis_index("col")
    row_count = lax.axis_size(ROW)
    col_count = lax.axis_size("col")
    rates_up = lax.dynamic_index_in_dim(path_rate, col_index, 1, False)
    rates_down = lax.dynamic_index_in_dim(path_rate, row_index, 0, False)
    down_whole = lax.all_gather(w_down[0], "col", axis=0, tiled=True)
    up_whole = gathered_by_axis(w_up[0], ROW, 0)
    pre = jnp.dot(tokens, up_whole, preferred_element_type=jnp.float32) * inv_width
    hidden_act, slope_out = finish_forward(tokens, targets, pre, down_whole, inv_hidden)
    slope_hidden = jnp.dot(slope_out, down_whole, preferred_element_type=jnp.float32) * inv_hidden
    slope_pre = (slope_hidden * silu_slope(pre)).astype(jnp.bfloat16)
    flags_up = lax.dynamic_index_in_dim(member_up, col_index, 1, False).astype(jnp.float32)
    weights_up = flags_up / jnp.sum(flags_up)
    input_parts = lax.all_to_all(
        tokens.reshape(rows, row_count, width // row_count),
        ROW,
        split_axis=1,
        concat_axis=1,
        tiled=True,
    )
    slope_parts = collect(slope_pre[None], ROW, 0)
    grads_owned = (
        jnp.einsum("rsk,srh->skh", input_parts, slope_parts, preferred_element_type=jnp.float32)
        * inv_width
    )
    quant_owned, scales_owned = packed(grads_owned, rates_up[:, None])
    average_up = owner_sum(weights_up, (quant_owned, scales_owned))
    momentum_first = 0.9 * up_momentum[0] + average_up
    fresh_up = (w_up[0].astype(jnp.float32) - 0.7 * (average_up + 0.9 * momentum_first)).astype(
        jnp.bfloat16
    )
    fresh_whole = gathered_by_axis(fresh_up, ROW, 0)
    pre_again = jnp.dot(tokens, fresh_whole, preferred_element_type=jnp.float32) * inv_width
    hidden_again, slope_again = finish_forward(tokens, targets, pre_again, down_whole, inv_hidden)
    flags_down = lax.dynamic_index_in_dim(member_down, row_index, 0, False).astype(jnp.float32)
    weights_down = flags_down / jnp.sum(flags_down)
    output_parts = lax.all_to_all(
        slope_again.reshape(rows, col_count, width // col_count),
        "col",
        split_axis=1,
        concat_axis=1,
        tiled=True,
    )
    hidden_parts = lax.all_gather(hidden_again[None], "col", axis=0, tiled=True)
    grads_down = (
        jnp.einsum("rsk,srh->skh", output_parts, hidden_parts, preferred_element_type=jnp.float32)
        * inv_hidden
    )
    quant_down, scales_down = packed(grads_down, rates_down[:, None])
    average_down = owner_sum(weights_down, (quant_down, scales_down))
    momentum_second = 0.9 * down_momentum[0] + average_down
    fresh_down = (
        w_down[0].astype(jnp.float32) - 0.7 * (average_down + 0.9 * momentum_second)
    ).astype(jnp.bfloat16)
    return (fresh_up[None], momentum_first[None], fresh_down[None], momentum_second[None])


def solution(mesh):
    torus = Mesh(mesh.devices.reshape(8, 2, mesh.shape["col"]), ("row_0", "row_1", "col"))
    placed = (
        P(ROW_COL, None),
        P(ROW_COL, None),
        P("col", ROW, None),
        P(ROW, "col", None),
        P("col", ROW, None),
        P(ROW, "col", None),
        P(),
        P(),
        P(),
    )
    return jax.shard_map(
        per_device,
        mesh=torus,
        in_specs=placed,
        out_specs=(
            P("col", ROW, None),
            P("col", ROW, None),
            P(ROW, "col", None),
            P(ROW, "col", None),
        ),
        check_vma=False,
    )
```

profile of v0, /device:TPU:1, one launch (start us, length us, event | category | flops | bytes accessed | tf_op | source)
XLA Modules:
  0.0 421.4 jit_solution(14377181742692491667)
XLA Ops:
  7.2 8.2 %all-gather = bf16[1,448,448]{2,1,0:T(8,128)(2,1)} all-gather(bf16[1,224,448]{2,1,0:T(8,128)(2,1)} %param.11), channel_id=2, replica_groups=mesh['row_0'=8,'row_1'=2,'col'=32] {'row_1'}, dimensions={1}, use_global_device_ids=true | all-gather | bytes 602112 | tf_op jit(solution)/shard_map/all_gather | solution.py:14
  16.2 2.2 copy.27
  18.4 8.8 %all-to-all-start.1 = ((bf16[128,16,224]{0,2,1:T(8,128)(2,1)}), bf16[128,16,224]{0,2,1:T(8,128)(2,1)S(1)}, u32[]{:S(2)}, u32[]{:S(2)}) async-start(bf16[128,16,224]{0,2,1:T(8,128)(2,1)} %bitcast.3), calls=%async_computation.1 | async-start | bytes 1835008 | tf_op jit(solution)/shard_map/all_to_all | solution.py:87
  27.3 58.7 %all-gather.11.cloned.1.call-done = bf16[1,3584,448]{2,1,0:T(8,128)(2,1)} async-done(((bf16[1,448,448]{2,1,0:T(8,128)(2,1)}), bf16[1,3584,448]{2,1,0:T(8,128)(2,1)}) %all-gather.11.cloned.1.call-update) | async-done | bytes 3211280 | tf_op jit(solution)/shard_map/all_gather | solution.py:14
  86.0 3.8 fusion.25
  89.8 93.1 %all-gather.13.cloned.1.call-done = bf16[1,3584,448]{2,1,0:T(8,128)(2,1)} async-done(((bf16[1,112,448]{2,1,0:T(8,128)(2,1)}), bf16[1,3584,448]{2,1,0:T(8,128)(2,1)}) %all-gather.13.cloned.1.call-update) | async-done | bytes 3211280 | tf_op jit(solution)/shard_map/all_gather | solution.py:79
  182.9 5.3 %fusion.39 = bf16[128,448]{0,1:T(8,128)(2,1)S(1)} fusion(bf16[1,3584,448]{2,1,0:T(8,128)(2,1)} %all-gather.13.cloned.1.call-done, bf16[128,3584]{1,0:T(8,128)(2,1)S(1)} %copy-done.2, bf16[128,3584]{1,0:T(8,128)(2,1)S(1)} %copy-done, f32[128,448]{0,1:T(8,128)S(1)} %fusion.25), kind=kOutput, calls=%fused_computation.40 | convolution fusion | flops 825696256 | bytes 5390336 | tf_op jit(solution)/shard_map/dot_general | solution.py:83
  188.3 1.6 broadcast_in_dim.4
  189.9 6.6 %all-to-all-start = ((bf16[16,1,128,448]{2,3,1,0:T(8,128)(2,1)}), bf16[16,1,128,448]{2,3,1,0:T(8,128)(2,1)S(1)}, u32[]{:S(2)}, u32[]{:S(2)}) async-start(bf16[16,1,128,448]{2,3,1,0:T(8,128)(2,1)} %broadcast_in_dim.4), calls=%async_computation | async-start | bytes 3670016 | tf_op jit(solution)/shard_map/all_to_all | solution.py:26
  196.5 1.1 copy.26
  197.6 1.2 copy.28
  199.5 0.8 dynamic-slice_reduce_fusion
  200.3 39.1 %all-to-all-done = bf16[16,1,128,448]{2,3,1,0:T(8,128)(2,1)S(1)} async-done(((bf16[16,1,128,448]{2,3,1,0:T(8,128)(2,1)}), bf16[16,1,128,448]{2,3,1,0:T(8,128)(2,1)S(1)}, u32[]{:S(2)}, u32[]{:S(2)}) %all-to-all-start) | async-done | bytes 1835040 | tf_op jit(solution)/shard_map/all_to_all | solution.py:26
  239.4 2.3 fusion.2
  241.7 2.0 fusion.5
  243.8 2.4 multiply_reduce_fusion.2
  246.5 5.7 %all_gather.21 = bf16[448,448]{1,0:T(8,128)(2,1)} all-gather(bf16[224,448]{1,0:T(8,128)(2,1)S(1)} %copy.29), channel_id=1, replica_groups=mesh['row_0'=8,'row_1'=2,'col'=32] {'row_1'}, dimensions={0}, use_global_device_ids=true | all-gather | bytes 602112 | tf_op jit(solution)/shard_map/all_gather | solution.py:14
  252.4 50.7 %all-gather.9.cloned.1.call-done = bf16[3584,448]{1,0:T(8,128)(2,1)} async-done(((bf16[448,448]{1,0:T(8,128)(2,1)}), bf16[3584,448]{1,0:T(8,128)(2,1)}) %all-gather.9.cloned.1.call-update) | async-done | bytes 3211280 | tf_op jit(solution)/shard_map/all_gather | solution.py:14
  303.1 4.0 multiply_convert_fusion
  307.1 3.7 fusion.11
  310.9 1.3 copy.30
  312.2 10.6 %all-to-all-start.2 = ((bf16[128,32,112]{0,2,1:T(8,128)(2,1)}), bf16[128,32,112]{0,2,1:T(8,128)(2,1)S(1)}, u32[]{:S(2)}, u32[]{:S(2)}) async-start(bf16[128,32,112]{0,2,1:T(8,128)(2,1)} %bitcast.114), calls=%async_computation.2 | async-start | bytes 1835008 | tf_op jit(solution)/shard_map/all_to_all | solution.py:110
  322.8 1.3 fusion.68
  324.1 1.3 fusion.67
  325.6 0.8 copy.32
  326.4 1.0 copy.33
  327.3 25.0 %all-to-all-done.2 = bf16[128,32,112]{0,2,1:T(8,128)(2,1)S(1)} async-done(((bf16[128,32,112]{0,2,1:T(8,128)(2,1)}), bf16[128,32,112]{0,2,1:T(8,128)(2,1)S(1)}, u32[]{:S(2)}, u32[]{:S(2)}) %all-to-all-start.2) | async-done | bytes 917536 | tf_op jit(solution)/shard_map/all_to_all | solution.py:110
  352.4 51.8 %all-gather.15.cloned.1.call-done = bf16[4096,448]{0,1:T(8,128)(2,1)} async-done(((bf16[128,448]{0,1:T(8,128)(2,1)}), bf16[4096,448]{0,1:T(8,128)(2,1)}) %all-gather.15.cloned.1.call-update) | async-done | bytes 3670032 | tf_op jit(solution)/shard_map/all_gather | solution.py:117
  404.2 3.8 multiply_reduce_fusion.1
  408.0 3.1 abs_reduce_fusion
  411.2 2.8 multiply_reduce_fusion
  414.0 0.8 fusion.54
  (31 shorter events, 2.4 us)
Async XLA Ops:
  7.2 175.8 %copy-start = (bf16[128,3584]{1,0:T(8,128)(2,1)S(1)}, bf16[128,3584]{1,0:T(8,128)(2,1)}, u32[]{:S(2)}) copy-start(bf16[128,3584]{1,0:T(8,128)(2,1)} %param.9) | copy-start | bytes 2752516
  7.2 175.8 %copy-start.2 = (bf16[128,3584]{1,0:T(8,128)(2,1)S(1)}, bf16[128,3584]{1,0:T(8,128)(2,1)}, u32[]{:S(2)}) copy-start(bf16[128,3584]{1,0:T(8,128)(2,1)} %param.10) | copy-start | bytes 2752516
  7.2 78.8 %all-gather.11.cloned.1.call-start = ((), (), s32[]{:S(2)}) async-start(), calls=%async_computation.4 | async-start | bytes 4128768 | tf_op jit(solution)/shard_map/all_gather | solution.py:14
  15.5 167.5 %all-gather.13.cloned.1.call-start = ((), (), s32[]{:S(2)}) async-start(), calls=%async_computation.5 | async-start | bytes 3784704 | tf_op jit(solution)/shard_map/all_gather | solution.py:79
  18.4 169.8 %all-to-all-start.1 = ((bf16[128,16,224]{0,2,1:T(8,128)(2,1)}), bf16[128,16,224]{0,2,1:T(8,128)(2,1)S(1)}, u32[]{:S(2)}, u32[]{:S(2)}) async-start(bf16[128,16,224]{0,2,1:T(8,128)(2,1)} %bitcast.3), calls=%async_computation.1 | async-start | bytes 1835008 | tf_op jit(solution)/shard_map/all_to_all | solution.py:87
  89.8 109.0 %copy-start.5 = (s32[16,32]{1,0:T(8,128)S(1)}, s32[16,32]{1,0:T(8,128)}, u32[]{:S(2)}) copy-start(s32[16,32]{1,0:T(8,128)} %param.15) | copy-start | bytes 6148
  89.8 109.7 %copy-start.6 = (f32[16,32]{1,0:T(8,128)S(1)}, f32[16,32]{1,0:T(8,128)}, u32[]{:S(2)}) copy-start(f32[16,32]{1,0:T(8,128)} %param.17) | copy-start | bytes 6148
  188.3 1.6 copy-start.1
  189.9 49.5 %all-to-all-start = ((bf16[16,1,128,448]{2,3,1,0:T(8,128)(2,1)}), bf16[16,1,128,448]{2,3,1,0:T(8,128)(2,1)S(1)}, u32[]{:S(2)}, u32[]{:S(2)}) async-start(bf16[16,1,128,448]{2,3,1,0:T(8,128)(2,1)} %broadcast_in_dim.4), calls=%async_computation | async-start | bytes 3670016 | tf_op jit(solution)/shard_map/all_to_all | solution.py:26
  196.4 106.7 %all-gather.9.cloned.1.call-start = ((), (), s32[]{:S(2)}) async-start(), calls=%async_computation.3 | async-start | bytes 4128768 | tf_op jit(solution)/shard_map/all_gather | solution.py:14
  252.2 152.0 %all-gather.15.cloned.1.call-start = ((), (), s32[]{:S(2)}) async-start(), calls=%async_computation.6 | async-start | bytes 3784704 | tf_op jit(solution)/shard_map/all_gather | solution.py:117
  312.2 40.2 %all-to-all-start.2 = ((bf16[128,32,112]{0,2,1:T(8,128)(2,1)}), bf16[128,32,112]{0,2,1:T(8,128)(2,1)S(1)}, u32[]{:S(2)}, u32[]{:S(2)}) async-start(bf16[128,32,112]{0,2,1:T(8,128)(2,1)} %bitcast.114), calls=%async_computation.2 | async-start | bytes 1835008 | tf_op jit(solution)/shard_map/all_to_all | solution.py:110
  408.0 6.1 %copy-start.3 = (bf16[1,112,448]{2,1,0:T(8,128)(2,1)S(1)}, bf16[1,112,448]{2,1,0:T(8,128)(2,1)}, u32[]{:S(2)}) copy-start(bf16[1,112,448]{2,1,0:T(8,128)(2,1)} %param.12) | copy-start | bytes 301060
  408.0 6.1 %copy-start.4 = (f32[1,112,448]{2,1,0:T(8,128)S(1)}, f32[1,112,448]{2,1,0:T(8,128)}, u32[]{:S(2)}) copy-start(f32[1,112,448]{2,1,0:T(8,128)} %param.14) | copy-start | bytes 602116
Sparse Core Ops, SparseCore 0:
  15.6 70.3 all-gather.10
  89.3 93.5 all-gather.12
  252.3 50.7 all-gather.8
  307.3 96.8 all-gather.14
where the time goes:
time: 422 us; the launch traced here: 421 us
  waiting for transfers between devices  319 us (76%)
  starting transfers between devices  26.4 us (6%)
  matrix products  23 us (5%)
  other arithmetic  15.7 us (4%)
  between operations  14 us (3%)
  blocking collectives  13.9 us (3%)
  local copies, waits for them, and re-layouts  9.32 us (2%)
    all_gather x2, waiting for transfers between devices, gathered_by_axis(): filled = lax.all_gather(filled, axes[number], axis=dim, tiled=True)  109 us
    all_gather x1, waiting for transfers between devices, per_device(): down_whole = lax.all_gather(w_down[0], 'col', axis=0, tiled=True)  93.1 us
    all_gather x1, waiting for transfers between devices, per_device(): hidden_parts = lax.all_gather(hidden_again[None], 'col', axis=0, tiled=True)  51.8 us
    all_to_all x1, waiting for transfers between devices, from_everyone(): lax.all_to_all(jnp.broadcast_to(x[None], (peers, *x.shape)), axis, 0, 0,...  39.1 us
    all_to_all x1, waiting for transfers between devices, per_device(): lax.all_to_all(slope_again.reshape(rows, col_count, width // col_count),...  25 us
    all_gather x2, blocking collectives, gathered_by_axis(): filled = lax.all_gather(filled, axes[number], axis=dim, tiled=True)  13.9 us
    all_to_all x1, starting transfers between devices, per_device(): lax.all_to_all(slope_again.reshape(rows, col_count, width // col_count),...  10.6 us
    all_to_all x1, starting transfers between devices, per_device(): lax.all_to_all(tokens.reshape(rows, row_count, width // row_count), ROW,...  8.84 us
  transfers between devices with their start and end apart: 7, of which 6 were waited for; matrix products, arithmetic and copies ran while one was open for 6% of the time, Pallas kernels for 0%

commit v1 on v0

--- a/solution.py
+++ b/solution.py
@@ -76,7 +76,9 @@
     col_count = lax.axis_size("col")
     rates_up = lax.dynamic_index_in_dim(path_rate, col_index, 1, False)
     rates_down = lax.dynamic_index_in_dim(path_rate, row_index, 0, False)
-    down_whole = lax.all_gather(w_down[0], "col", axis=0, tiled=True)
+    down_whole = jnp.concatenate(
+        lax.all_to_all(jnp.stack([w_down[0]] * lax.axis_size("col")), "col", 0, 0), axis=0
+    )
     up_whole = gathered_by_axis(w_up[0], ROW, 0)
     pre = jnp.dot(tokens, up_whole, preferred_element_type=jnp.float32) * inv_width
     hidden_act, slope_out = finish_forward(tokens, targets, pre, down_whole, inv_hidden)

time: 422 us -> 374 us (0.89)
  waiting for transfers between devices: 319 us -> 250 us
  starting transfers between devices: 26.4 us -> 38.4 us
  blocking collectives: 13.9 us -> 21.4 us
    all_gather x1 -> x0, waiting for transfers between devices: 93.1 us -> none  [per_device(): down_whole = lax.all_gather(w_down[0], 'col', axis=0, tiled=True)]
    all_to_all x0 -> x1, waiting for transfers between devices: none -> 67.8 us  [per_device(): lax.all_to_all(jnp.stack([w_down[0]] * lax.axis_size('col')), 'col', 0, 0)]
    all_gather x2, waiting for transfers between devices: 109 us -> 53 us  [gathered_by_axis(): filled = lax.all_gather(filled, axes[number], axis=dim, tiled=True)]
    all_to_all x0 -> x1, starting transfers between devices: none -> 14.6 us  [per_device(): lax.all_to_all(jnp.stack([w_down[0]] * lax.axis_size('col')), 'col', 0, 0)]
    all_to_all x1, waiting for transfers between devices: 0.01 us -> 14 us  [per_device(): lax.all_to_all(tokens.reshape(rows, row_count, width // row_count), ROW,...]
    all_gather x2, blocking collectives: 13.9 us -> 21.4 us  [gathered_by_axis(): filled = lax.all_gather(filled, axes[number], axis=dim, tiled=True)]
where the time goes in v1:
time: 374 us
  waiting for transfers between devices  250 us (67%)
  starting transfers between devices  38.4 us (10%)
  matrix products  22.7 us (6%)
  blocking collectives  21.4 us (6%)
  other arithmetic  15.6 us (4%)
  between operations  14 us (4%)
  local copies, waits for them, and re-layouts  11.6 us (3%)
    all_to_all x1, waiting for transfers between devices, per_device(): lax.all_to_all(jnp.stack([w_down[0]] * lax.axis_size('col')), 'col', 0, 0)  67.8 us
    all_gather x2, waiting for transfers between devices, gathered_by_axis(): filled = lax.all_gather(filled, axes[number], axis=dim, tiled=True)  53 us
    all_gather x1, waiting for transfers between devices, per_device(): hidden_parts = lax.all_gather(hidden_again[None], 'col', axis=0, tiled=True)  51.8 us
    all_to_all x1, waiting for transfers between devices, from_everyone(): lax.all_to_all(jnp.broadcast_to(x[None], (peers, *x.shape)), axis, 0, 0,...  38 us
    all_to_all x1, waiting for transfers between devices, per_device(): lax.all_to_all(slope_again.reshape(rows, col_count, width // col_count),...  25 us
    all_gather x2, blocking collectives, gathered_by_axis(): filled = lax.all_gather(filled, axes[number], axis=dim, tiled=True)  21.4 us
    all_to_all x1, starting transfers between devices, per_device(): lax.all_to_all(jnp.stack([w_down[0]] * lax.axis_size('col')), 'col', 0, 0)  14.6 us
    all_to_all x1, waiting for transfers between devices, per_device(): lax.all_to_all(tokens.reshape(rows, row_count, width // row_count), ROW,...  14 us
  transfers between devices with their start and end apart: 7, of which 6 were waited for; matrix products, arithmetic and copies ran while one was open for 6% of the time, Pallas kernels for 0%

profile of v1, /device:TPU:1, one launch (start us, length us, event | category | flops | bytes accessed | tf_op | source)
XLA Modules:
  0.0 373.6 jit_solution(14454274645998363263)
XLA Ops:
  7.2 3.2 stack.3
  10.4 14.6 %all-to-all-start = ((bf16[32,112,448]{2,1,0:T(8,128)(2,1)}), bf16[32,112,448]{2,1,0:T(8,128)(2,1)}, u32[]{:S(2)}, u32[]{:S(2)}) async-start(bf16[32,112,448]{2,1,0:T(8,128)(2,1)} %stack.3), calls=%async_computation | async-start | bytes 7340032 | tf_op jit(solution)/shard_map/all_to_all | solution.py:80
  25.1 15.8 %all-gather = bf16[1,448,448]{2,1,0:T(8,128)(2,1)} all-gather(bf16[1,224,448]{2,1,0:T(8,128)(2,1)S(1)} %copy-done.3), channel_id=2, replica_groups=mesh['row_0'=8,'row_1'=2,'col'=32] {'row_1'}, dimensions={1}, use_global_device_ids=true | all-gather | bytes 602112 | tf_op jit(solution)/shard_map/all_gather | solution.py:14
  40.9 1.3 copy.27
  42.2 67.8 %all-to-all-done = bf16[32,112,448]{2,1,0:T(8,128)(2,1)} async-done(((bf16[32,112,448]{2,1,0:T(8,128)(2,1)}), bf16[32,112,448]{2,1,0:T(8,128)(2,1)}, u32[]{:S(2)}, u32[]{:S(2)}) %all-to-all-start) | async-done | bytes 3211296 | tf_op jit(solution)/shard_map/all_to_all | solution.py:80
  110.0 7.0 %all-to-all-start.2 = ((bf16[128,16,224]{0,2,1:T(8,128)(2,1)}), bf16[128,16,224]{0,2,1:T(8,128)(2,1)S(1)}, u32[]{:S(2)}, u32[]{:S(2)}) async-start(bf16[128,16,224]{0,2,1:T(8,128)(2,1)} %bitcast.4), calls=%async_computation.2 | async-start | bytes 1835008 | tf_op jit(solution)/shard_map/all_to_all | solution.py:89
  117.0 3.5 fusion.19
  120.6 5.3 %fusion.24 = bf16[128,448]{0,1:T(8,128)(2,1)S(1)} fusion(bf16[3584,448]{1,0:T(8,128)(2,1)} %bitcast.2, bf16[128,3584]{1,0:T(8,128)(2,1)S(1)} %copy-done.2, bf16[128,3584]{1,0:T(8,128)(2,1)S(1)} %copy-done, f32[128,448]{0,1:T(8,128)S(1)} %fusion.19), kind=kOutput, calls=%fused_computation.36 | convolution fusion | flops 825696256 | bytes 5390336 | tf_op jit(solution)/shard_map/dot_general | solution.py:85
  125.9 14.0 %all-to-all-done.2 = bf16[128,16,224]{0,2,1:T(8,128)(2,1)S(1)} async-done(((bf16[128,16,224]{0,2,1:T(8,128)(2,1)}), bf16[128,16,224]{0,2,1:T(8,128)(2,1)S(1)}, u32[]{:S(2)}, u32[]{:S(2)}) %all-to-all-start.2) | async-done | bytes 917536 | tf_op jit(solution)/shard_map/all_to_all | solution.py:89
  139.9 1.6 broadcast_in_dim.4
  141.5 5.9 %all-to-all-start.1 = ((bf16[16,1,128,448]{2,3,1,0:T(8,128)(2,1)}), bf16[16,1,128,448]{2,3,1,0:T(8,128)(2,1)S(1)}, u32[]{:S(2)}, u32[]{:S(2)}) async-start(bf16[16,1,128,448]{2,3,1,0:T(8,128)(2,1)} %broadcast_in_dim.4), calls=%async_computation.1 | async-start | bytes 3670016 | tf_op jit(solution)/shard_map/all_to_all | solution.py:26
  147.5 1.1 copy.26
  148.6 1.2 copy.28
  150.5 0.8 dynamic-slice_reduce_fusion
  151.3 38.0 %all-to-all-done.1 = bf16[16,1,128,448]{2,3,1,0:T(8,128)(2,1)S(1)} async-done(((bf16[16,1,128,448]{2,3,1,0:T(8,128)(2,1)}), bf16[16,1,128,448]{2,3,1,0:T(8,128)(2,1)S(1)}, u32[]{:S(2)}, u32[]{:S(2)}) %all-to-all-start.1) | async-done | bytes 1835040 | tf_op jit(solution)/shard_map/all_to_all | solution.py:26
  189.3 2.3 fusion.2
  191.7 2.0 fusion.5
  193.8 2.4 multiply_reduce_fusion.2
  196.4 5.7 %all_gather.17 = bf16[448,448]{1,0:T(8,128)(2,1)} all-gather(bf16[224,448]{1,0:T(8,128)(2,1)S(1)} %copy.29), channel_id=1, replica_groups=mesh['row_0'=8,'row_1'=2,'col'=32] {'row_1'}, dimensions={0}, use_global_device_ids=true | all-gather | bytes 602112 | tf_op jit(solution)/shard_map/all_gather | solution.py:14
  202.3 53.0 %all-gather.7.cloned.1.call-done = bf16[3584,448]{1,0:T(8,128)(2,1)} async-done(((bf16[448,448]{1,0:T(8,128)(2,1)}), bf16[3584,448]{1,0:T(8,128)(2,1)}) %all-gather.7.cloned.1.call-update) | async-done | bytes 3211280 | tf_op jit(solution)/shard_map/all_gather | solution.py:14
  255.3 4.0 %multiply_convert_fusion = bf16[128,448]{0,1:T(8,128)(2,1)} fusion(bf16[3584,448]{1,0:T(8,128)(2,1)} %all-gather.7.cloned.1.call-done, bf16[128,3584]{1,0:T(8,128)(2,1)S(1)} %copy-done), kind=kOutput, calls=%fused_computation.55 | convolution fusion | flops 411385856 | bytes 4243456 | tf_op jit(solution)/shard_map/dot_general | solution.py:108
  259.4 3.7 fusion.11
  263.1 1.3 copy.30
  264.4 10.6 %all-to-all-start.3 = ((bf16[128,32,112]{0,2,1:T(8,128)(2,1)}), bf16[128,32,112]{0,2,1:T(8,128)(2,1)S(1)}, u32[]{:S(2)}, u32[]{:S(2)}) async-start(bf16[128,32,112]{0,2,1:T(8,128)(2,1)} %bitcast.98), calls=%async_computation.3 | async-start | bytes 1835008 | tf_op jit(solution)/shard_map/all_to_all | solution.py:112
  275.0 1.3 fusion.49
  276.3 1.3 fusion.48
  278.6 1.0 copy.33
  279.6 25.0 %all-to-all-done.3 = bf16[128,32,112]{0,2,1:T(8,128)(2,1)S(1)} async-done(((bf16[128,32,112]{0,2,1:T(8,128)(2,1)}), bf16[128,32,112]{0,2,1:T(8,128)(2,1)S(1)}, u32[]{:S(2)}, u32[]{:S(2)}) %all-to-all-start.3) | async-done | bytes 917536 | tf_op jit(solution)/shard_map/all_to_all | solution.py:112
  304.6 51.8 %all-gather.11.cloned.1.call-done = bf16[4096,448]{0,1:T(8,128)(2,1)} async-done(((bf16[128,448]{0,1:T(8,128)(2,1)}), bf16[4096,448]{0,1:T(8,128)(2,1)}) %all-gather.11.cloned.1.call-update) | async-done | bytes 3670032 | tf_op jit(solution)/shard_map/all_gather | solution.py:119
  356.4 3.8 %multiply_reduce_fusion.1 = (f32[32,112]{1,0:T(8,128)S(1)}, f32[32,112,448]{2,1,0:T(8,128)S(1)}) fusion(bf16[128,32,112]{0,2,1:T(8,128)(2,1)S(1)} %all-to-all-done.3, bf16[4096,448]{0,1:T(8,128)(2,1)} %all-gather.11.cloned.1.call-done), kind=kOutput, calls=%fused_computation.11 | convolution fusion | flops 415855104 | bytes 11024384 | tf_op jit(solution)/shard_map/rsk,srh->skh/dot_general | solution.py:121
  360.2 3.1 abs_reduce_fusion
  363.4 2.8 multiply_reduce_fusion
  (33 shorter events, 3.2 us)
Async XLA Ops:
  7.2 17.9 %copy-start.3 = (bf16[1,224,448]{2,1,0:T(8,128)(2,1)S(1)}, bf16[1,224,448]{2,1,0:T(8,128)(2,1)}, u32[]{:S(2)}) copy-start(bf16[1,224,448]{2,1,0:T(8,128)(2,1)} %param.11) | copy-start | bytes 602116
  7.2 33.7 %copy-start = (bf16[128,3584]{1,0:T(8,128)(2,1)S(1)}, bf16[128,3584]{1,0:T(8,128)(2,1)}, u32[]{:S(2)}) copy-start(bf16[128,3584]{1,0:T(8,128)(2,1)} %param.9) | copy-start | bytes 2752516
  10.4 110.1 %copy-start.2 = (bf16[128,3584]{1,0:T(8,128)(2,1)S(1)}, bf16[128,3584]{1,0:T(8,128)(2,1)}, u32[]{:S(2)}) copy-start(bf16[128,3584]{1,0:T(8,128)(2,1)} %param.10) | copy-start | bytes 2752516
  10.4 99.6 %all-to-all-start = ((bf16[32,112,448]{2,1,0:T(8,128)(2,1)}), bf16[32,112,448]{2,1,0:T(8,128)(2,1)}, u32[]{:S(2)}, u32[]{:S(2)}) async-start(bf16[32,112,448]{2,1,0:T(8,128)(2,1)} %stack.3), calls=%async_computation | async-start | bytes 7340032 | tf_op jit(solution)/shard_map/all_to_all | solution.py:80
  25.0 91.9 %all-gather.9.cloned.1.call-start = ((), (), s32[]{:S(2)}) async-start(), calls=%async_computation.5 | async-start | bytes 4128768 | tf_op jit(solution)/shard_map/all_gather | solution.py:14
  110.0 29.9 %all-to-all-start.2 = ((bf16[128,16,224]{0,2,1:T(8,128)(2,1)}), bf16[128,16,224]{0,2,1:T(8,128)(2,1)S(1)}, u32[]{:S(2)}, u32[]{:S(2)}) async-start(bf16[128,16,224]{0,2,1:T(8,128)(2,1)} %bitcast.4), calls=%async_computation.2 | async-start | bytes 1835008 | tf_op jit(solution)/shard_map/all_to_all | solution.py:89
  120.5 29.2 %copy-start.6 = (s32[16,32]{1,0:T(8,128)S(1)}, s32[16,32]{1,0:T(8,128)}, u32[]{:S(2)}) copy-start(s32[16,32]{1,0:T(8,128)} %param.15) | copy-start | bytes 6148
  120.5 29.9 %copy-start.7 = (f32[16,32]{1,0:T(8,128)S(1)}, f32[16,32]{1,0:T(8,128)}, u32[]{:S(2)}) copy-start(f32[16,32]{1,0:T(8,128)} %param.17) | copy-start | bytes 6148
  139.9 1.6 copy-start.1
  141.5 47.8 %all-to-all-start.1 = ((bf16[16,1,128,448]{2,3,1,0:T(8,128)(2,1)}), bf16[16,1,128,448]{2,3,1,0:T(8,128)(2,1)S(1)}, u32[]{:S(2)}, u32[]{:S(2)}) async-start(bf16[16,1,128,448]{2,3,1,0:T(8,128)(2,1)} %broadcast_in_dim.4), calls=%async_computation.1 | async-start | bytes 3670016 | tf_op jit(solution)/shard_map/all_to_all | solution.py:26
  147.4 107.9 %all-gather.7.cloned.1.call-start = ((), (), s32[]{:S(2)}) async-start(), calls=%async_computation.4 | async-start | bytes 4128768 | tf_op jit(solution)/shard_map/all_gather | solution.py:14
  202.1 154.3 %all-gather.11.cloned.1.call-start = ((), (), s32[]{:S(2)}) async-start(), calls=%async_computation.6 | async-start | bytes 3784704 | tf_op jit(solution)/shard_map/all_gather | solution.py:119
  264.4 40.2 %all-to-all-start.3 = ((bf16[128,32,112]{0,2,1:T(8,128)(2,1)}), bf16[128,32,112]{0,2,1:T(8,128)(2,1)S(1)}, u32[]{:S(2)}, u32[]{:S(2)}) async-start(bf16[128,32,112]{0,2,1:T(8,128)(2,1)} %bitcast.98), calls=%async_computation.3 | async-start | bytes 1835008 | tf_op jit(solution)/shard_map/all_to_all | solution.py:112
  360.2 6.0 %copy-start.4 = (bf16[1,112,448]{2,1,0:T(8,128)(2,1)S(1)}, bf16[1,112,448]{2,1,0:T(8,128)(2,1)}, u32[]{:S(2)}) copy-start(bf16[1,112,448]{2,1,0:T(8,128)(2,1)} %param.12) | copy-start | bytes 301060
  360.2 6.0 %copy-start.5 = (f32[1,112,448]{2,1,0:T(8,128)S(1)}, f32[1,112,448]{2,1,0:T(8,128)}, u32[]{:S(2)}) copy-start(f32[1,112,448]{2,1,0:T(8,128)} %param.14) | copy-start | bytes 602116
Sparse Core Ops, SparseCore 0:
  41.0 59.7 all-gather.8
  202.2 53.0 all-gather.6
  259.5 96.8 all-gather.10
